TPU v7x, 32 devices: a whole 2x2x4 slice. The times are simulated.
32 devices in a mesh: row: 8 (over y, x, core), col: 4 (over z).
Axes of the slice: x: 2, y: 2, z: 4, core: 2. Of those that a mesh axis runs over, the one named last changes fastest.
Arguments:
- treated: bfloat16 [8192, 64], P('row'), may hold values from -6 to 6
- donors: bfloat16 [32768, 64], P('col'), may hold values from -6 to 6
- treated_counts: int32 [8192], P('row'), may hold values from 1 to 95, as said below
- donor_counts: int32 [32768], P('col'), may hold values from 1 to 95, as said below
Outputs:
- treated_dual: float32 [8192], P('row')
- donor_dual: float32 [32768], P('col')
Inputs may be any that keep to these rules, and one draw needn't show every extreme that they name: `treated_counts`: positive region multiplicities. `donor_counts`: positive region multiplicities.
All inputs are finite; a program needn't handle non-finite values.
Results may differ from a plain program's by a relative error of at most 0.0003.
Values sent between devices are 32-bit elements; how exact they have to be, the bound alone decides.
A program may use at most 64 MiB of HBM per device.

v0:
```python
import jax
import jax.numpy as jnp
from jax import lax
from jax.sharding import PartitionSpec as P

ITERS = 4


entropic = 0.5


def merged(value, axis, combine):
    everything = jax.tree.map(lambda part: lax.all_gather(part, axis), value)
    initial = jax.tree.map(lambda part: part[0], everything)

    def hop(k, so_far):
        return combine(so_far, jax.tree.map(lambda part: part[k], everything))

    return lax.fori_loop(1, lax.axis_size(axis), hop, initial)


def partial_soft(points, others, others_term):
    rows_here = points.shape[0]
    cols_here = others.shape[0]
    width_here = points.shape[1]
    row_block = min(rows_here, 1024)
    col_block = min(cols_here, 4096)
    others_sq = jnp.sum(jnp.square(others.astype(jnp.float32)), axis=1)
    other_blocks = others.reshape(cols_here // col_block, col_block, width_here)
    square_blocks = others_sq.reshape(cols_here // col_block, col_block)
    term_blocks = others_term.reshape(cols_here // col_block, col_block)

    def one_rows(pieces):
        own_sq = jnp.sum(jnp.square(pieces.astype(jnp.float32)), axis=1)

        def step_cols(carry, items):
            highest, summed = carry
            cols_points, cols_square, cols_term = items
            products = jnp.einsum(
                "ak,bk->ab", pieces, cols_points, preferred_element_type=jnp.float32
            )
            distance = own_sq[:, None] + cols_square[None, :] - 2.0 * products
            scores = (cols_term[None, :] - distance) / entropic
            newest = jnp.maximum(highest, jnp.max(scores, axis=1))
            summed = summed * jnp.exp(highest - newest) + jnp.sum(
                jnp.exp(scores - newest[:, None]), axis=1
            )
            return ((newest, summed), None)

        starting = (
            jnp.full((row_block,), -jnp.inf, jnp.float32),
            jnp.zeros((row_block,), jnp.float32),
        )
        finished, unused = lax.scan(step_cols, starting, (other_blocks, square_blocks, term_blocks))
        return finished

    highest, summed = lax.map(
        one_rows, points.reshape(rows_here // row_block, row_block, width_here)
    )
    return (highest.reshape(rows_here), summed.reshape(rows_here))


def combine_parts(earlier, later):
    newest = jnp.maximum(earlier[0], later[0])
    return (
        newest,
        earlier[1] * jnp.exp(earlier[0] - newest) + later[1] * jnp.exp(later[0] - newest),
    )


def on_device(treated, donors, treated_counts, donor_counts):
    treated_float = treated_counts.astype(jnp.float32)
    donor_float = donor_counts.astype(jnp.float32)
    treated_total = lax.psum(jnp.sum(treated_float), "row")
    donor_total = lax.psum(jnp.sum(donor_float), "col")
    treated_log = jnp.log(treated_float) - jnp.log(treated_total)
    donor_log = jnp.log(donor_float) - jnp.log(donor_total)
    donor_dual = jnp.zeros((donors.shape[0],), jnp.float32)
    treated_dual = jnp.zeros((treated.shape[0],), jnp.float32)
    for sweep in range(ITERS):
        highest, summed = partial_soft(treated, donors, donor_dual + entropic * donor_log)
        ceiling = lax.pmax(highest, "col")
        summed = lax.psum(summed * jnp.exp(highest - ceiling), "col")
        highest = ceiling
        treated_dual = -entropic * (highest + jnp.log(summed))
        highest, summed = partial_soft(donors, treated, treated_dual + entropic * treated_log)
        highest, summed = merged((highest, summed), "row", combine_parts)
        donor_dual = -entropic * (highest + jnp.log(summed))
    return (treated_dual, donor_dual)


def solution(mesh):
    in_specs = (P("row", None), P("col", None), P("row"), P("col"))
    out_specs = (P("row"), P("col"))
    return jax.shard_map(
        on_device, mesh=mesh, in_specs=in_specs, out_specs=out_specs, check_vma=False
    )
```

profile of v0, /device:TPU:0, one launch (start us, length us, event | category | flops | bytes accessed | tf_op | source)
XLA Modules:
  0.0 419.8 jit_solution(15408120286920875432)
XLA Ops:
  0.6 2.1 copy.9
  5.0 14.1 %psum.42 = f32[]{:T(128)} all-reduce(f32[]{:T(128)} %convert_reduce_fusion), channel_id=1, replica_groups=mesh['row'=8,'col'=4] {'col'}, use_global_device_ids=true, to_apply=%region_3.0 | all-reduce | flops 1 | bytes 8 | tf_op jit(solution)/shard_map/psum | solution.py:75
  22.1 31.2 %while.232 = (s32[]{:T(128)}, f32[1024]{0:T(1024)S(1)}, f32[1024]{0:T(1024)S(1)}, f32[2,4096]{1,0:T(2,128)S(1)}, f32[1024]{0:T(1024)S(1)}, /*index=5*/f32[2,4096...) while((s32[]{:T(128)}, f32[1024]{0:T(1024)S(1)}, ...), condition=%wide.region_7.8_spmd.clone, body=%wide.region_4.7_spmd.clone.sunk | while | flops 591401984 | bytes 34926708 | solution.py:54
  22.2 7.0 %fusion.82 = (f32[1024]{0:T(1024)S(1)}, f32[4096,1024]{1,0:T(8,128)}) fusion(f32[4096]{0:T(1024)S(1)} %bitcast.331, f32[1024]{0:T(1024)S(1)} %get-tuple-element.1968, f32[4096]{0:T(1024)S(1)} %bitcast.333, bf16[1024,64]{0,1:T(8,128)(2,1)S(1)} %get-tuple-element.1971, bf16[2,4096,64]{2,1,0:T(8,128)(2,1)S(1)} %get-tuple-element.1970, ...), kind=kOutput, calls=%fused_computation.56.clone.1 | convolution fusion | flops 562035712 | bytes 17997828 | tf_op jit(solution)/shard_map/while/body/eval_jaxpr/while/body/eval_jaxpr/ak,bk->ab/dot_general | solution.py:39
  29.2 8.5 %exponential_reduce_fusion.20 = f32[1024]{0:T(1024)S(1)} fusion(f32[4096,1024]{1,0:T(8,128)} %get-tuple-element.1907, f32[1024]{0:T(1024)S(1)} %select_maximum_fusion.8, f32[4096]{0:T(1024)S(1)} %bitcast.332, f32[1024]{0:T(1024)S(1)} %get-tuple-element.1968, f32[4096]{0:T(1024)S(1)} %bitcast.334), kind=kLoop, calls=%fused_computation.55.clone.1 | loop fusion | flops 29359104 | bytes 16822272 | tf_op jit(solution)/shard_map/while/body/eval_jaxpr/while/body/eval_jaxpr/reduce_sum | solution.py:45
  37.8 7.0 %fusion.82 = (f32[1024]{0:T(1024)S(1)}, f32[4096,1024]{1,0:T(8,128)}) fusion(f32[4096]{0:T(1024)S(1)} %bitcast.331, f32[1024]{0:T(1024)S(1)} %get-tuple-element.1968, f32[4096]{0:T(1024)S(1)} %bitcast.333, bf16[1024,64]{0,1:T(8,128)(2,1)S(1)} %get-tuple-element.1971, bf16[2,4096,64]{2,1,0:T(8,128)(2,1)S(1)} %get-tuple-element.1970, ...), kind=kOutput, calls=%fused_computation.56.clone.1 | convolution fusion | flops 562035712 | bytes 17997828 | tf_op jit(solution)/shard_map/while/body/eval_jaxpr/while/body/eval_jaxpr/ak,bk->ab/dot_general | solution.py:39
  44.8 8.5 %exponential_reduce_fusion.20 = f32[1024]{0:T(1024)S(1)} fusion(f32[4096,1024]{1,0:T(8,128)} %get-tuple-element.1907, f32[1024]{0:T(1024)S(1)} %select_maximum_fusion.8, f32[4096]{0:T(1024)S(1)} %bitcast.332, f32[1024]{0:T(1024)S(1)} %get-tuple-element.1968, f32[4096]{0:T(1024)S(1)} %bitcast.334), kind=kLoop, calls=%fused_computation.55.clone.1 | loop fusion | flops 29359104 | bytes 16822272 | tf_op jit(solution)/shard_map/while/body/eval_jaxpr/while/body/eval_jaxpr/reduce_sum | solution.py:45
  53.4 8.4 %pmax.28 = f32[1024]{0:T(1024)S(1)} all-reduce(f32[1024]{0:T(1024)S(1)} %get-tuple-element.1038), channel_id=1, replica_groups=mesh['row'=8,'col'=4] {'col'}, use_global_device_ids=true, to_apply=%region_8.9 | all-reduce | flops 1024 | bytes 8192 | tf_op jit(solution)/shard_map/pmax | solution.py:82
  61.8 10.3 %psum.43 = f32[1024]{0:T(1024)S(1)} all-reduce(f32[1024]{0:T(1024)S(1)} %exponential_multiply_fusion.3), channel_id=1, replica_groups=mesh['row'=8,'col'=4] {'col'}, use_global_device_ids=true, to_apply=%region_9.10 | all-reduce | flops 1024 | bytes 8192 | tf_op jit(solution)/shard_map/psum | solution.py:83
  72.7 12.4 %psum.44 = f32[]{:T(128)} all-reduce(f32[]{:T(128)} %convert_reduce_fusion.1), channel_id=1, replica_groups=mesh['row'=8,'col'=4] {'row'}, use_global_device_ids=true, to_apply=%region_11.12 | all-reduce | flops 1 | bytes 8 | tf_op jit(solution)/shard_map/psum | solution.py:74
  86.1 26.6 %while.224 = (s32[]{:T(128)}, f32[8,1024]{1,0:T(8,128)S(1)}, f32[8,1024]{1,0:T(8,128)S(1)}, f32[1,1024]{1,0:T(1,128)S(1)}, bf16[8,1024,64]{2,1,0:T(8,128)(2,1)S(...) while((s32[]{:T(128)}, f32[8,1024]{1,0:T(8,128)S(1)}, ...), condition=%wide.region_16.17_spmd, body=%wide.region_12.16_spmd.sunk | while | flops 148045824 | bytes 9113709 | solution.py:57
  87.4 1.8 exponential_reduce_fusion.16
  97.3 1.8 exponential_reduce_fusion.16
  100.7 1.8 exponential_reduce_fusion.16
  107.3 1.8 exponential_reduce_fusion.16
  112.8 9.3 %all-gather.1 = f32[8,1,8192]{2,1,0:T(1,128)S(1)} all-gather(f32[1,1,8192]{2,1,0:T(1,128)S(1)} %reshape.191), channel_id=1, replica_groups=mesh['row'=8,'col'=4] {'row'}, dimensions={0}, use_global_device_ids=true | all-gather | bytes 294912 | tf_op jit(solution)/shard_map/all_gather | solution.py:13
  122.3 8.3 %all-gather = f32[8,1,8192]{2,1,0:T(1,128)S(1)} all-gather(f32[1,1,8192]{2,1,0:T(1,128)S(1)} %reshape.189), channel_id=1, replica_groups=mesh['row'=8,'col'=4] {'row'}, dimensions={0}, use_global_device_ids=true | all-gather | bytes 294912 | tf_op jit(solution)/shard_map/all_gather | solution.py:13
  131.7 31.2 %while.233 = (s32[]{:T(128)}, f32[1024]{0:T(1024)S(1)}, f32[1024]{0:T(1024)S(1)}, f32[2,4096]{1,0:T(2,128)S(1)}, f32[1024]{0:T(1024)S(1)}, /*index=5*/f32[2,4096...) while((s32[]{:T(128)}, f32[1024]{0:T(1024)S(1)}, ...), condition=%wide.region_22.23_spmd.clone, body=%wide.region_19.22_spmd.clone.sunk | while | flops 591401984 | bytes 34926708 | solution.py:54
  131.8 7.0 %fusion.85 = (f32[1024]{0:T(1024)S(1)}, f32[4096,1024]{1,0:T(8,128)}) fusion(f32[4096]{0:T(1024)S(1)} %bitcast.335, f32[1024]{0:T(1024)S(1)} %get-tuple-element.2049, f32[4096]{0:T(1024)S(1)} %bitcast.337, bf16[1024,64]{0,1:T(8,128)(2,1)S(1)} %get-tuple-element.2052, bf16[2,4096,64]{2,1,0:T(8,128)(2,1)S(1)} %get-tuple-element.2051, ...), kind=kOutput, calls=%fused_computation.70.clone.1 | convolution fusion | flops 562035712 | bytes 17997828 | tf_op jit(solution)/shard_map/while/body/eval_jaxpr/while/body/eval_jaxpr/ak,bk->ab/dot_general | solution.py:39
  138.8 8.5 %exponential_reduce_fusion.21 = f32[1024]{0:T(1024)S(1)} fusion(f32[4096,1024]{1,0:T(8,128)} %get-tuple-element.1919, f32[1024]{0:T(1024)S(1)} %select_maximum_fusion.9, f32[4096]{0:T(1024)S(1)} %bitcast.336, f32[1024]{0:T(1024)S(1)} %get-tuple-element.2049, f32[4096]{0:T(1024)S(1)} %bitcast.338), kind=kLoop, calls=%fused_computation.69.clone.1 | loop fusion | flops 29359104 | bytes 16822272 | tf_op jit(solution)/shard_map/while/body/eval_jaxpr/while/body/eval_jaxpr/reduce_sum | solution.py:45
  147.4 7.0 %fusion.85 = (f32[1024]{0:T(1024)S(1)}, f32[4096,1024]{1,0:T(8,128)}) fusion(f32[4096]{0:T(1024)S(1)} %bitcast.335, f32[1024]{0:T(1024)S(1)} %get-tuple-element.2049, f32[4096]{0:T(1024)S(1)} %bitcast.337, bf16[1024,64]{0,1:T(8,128)(2,1)S(1)} %get-tuple-element.2052, bf16[2,4096,64]{2,1,0:T(8,128)(2,1)S(1)} %get-tuple-element.2051, ...), kind=kOutput, calls=%fused_computation.70.clone.1 | convolution fusion | flops 562035712 | bytes 17997828 | tf_op jit(solution)/shard_map/while/body/eval_jaxpr/while/body/eval_jaxpr/ak,bk->ab/dot_general | solution.py:39
  154.4 8.5 %exponential_reduce_fusion.21 = f32[1024]{0:T(1024)S(1)} fusion(f32[4096,1024]{1,0:T(8,128)} %get-tuple-element.1919, f32[1024]{0:T(1024)S(1)} %select_maximum_fusion.9, f32[4096]{0:T(1024)S(1)} %bitcast.336, f32[1024]{0:T(1024)S(1)} %get-tuple-element.2049, f32[4096]{0:T(1024)S(1)} %bitcast.338), kind=kLoop, calls=%fused_computation.69.clone.1 | loop fusion | flops 29359104 | bytes 16822272 | tf_op jit(solution)/shard_map/while/body/eval_jaxpr/while/body/eval_jaxpr/reduce_sum | solution.py:45
  162.9 8.4 %pmax.29 = f32[1024]{0:T(1024)S(1)} all-reduce(f32[1024]{0:T(1024)S(1)} %get-tuple-element.1044), channel_id=1, replica_groups=mesh['row'=8,'col'=4] {'col'}, use_global_device_ids=true, to_apply=%region_23.24 | all-reduce | flops 1024 | bytes 8192 | tf_op jit(solution)/shard_map/pmax | solution.py:82
  171.3 10.4 %psum.45 = f32[1024]{0:T(1024)S(1)} all-reduce(f32[1024]{0:T(1024)S(1)} %exponential_multiply_fusion.2), channel_id=1, replica_groups=mesh['row'=8,'col'=4] {'col'}, use_global_device_ids=true, to_apply=%region_24.25 | all-reduce | flops 1024 | bytes 8192 | tf_op jit(solution)/shard_map/psum | solution.py:83
  181.7 26.6 %while.226 = (s32[]{:T(128)}, f32[8,1024]{1,0:T(8,128)S(1)}, f32[8,1024]{1,0:T(8,128)S(1)}, f32[1,1024]{1,0:T(1,128)S(1)}, bf16[8,1024,64]{2,1,0:T(8,128)(2,1)S(...) while((s32[]{:T(128)}, f32[8,1024]{1,0:T(8,128)S(1)}, ...), condition=%wide.region_29.30_spmd, body=%wide.region_25.29_spmd.sunk | while | flops 148045824 | bytes 9113709 | solution.py:57
  183.0 1.8 exponential_reduce_fusion.17
  208.4 9.3 %all-gather.3 = f32[8,1,8192]{2,1,0:T(1,128)S(1)} all-gather(f32[1,1,8192]{2,1,0:T(1,128)S(1)} %reshape.195), channel_id=1, replica_groups=mesh['row'=8,'col'=4] {'row'}, dimensions={0}, use_global_device_ids=true | all-gather | bytes 294912 | tf_op jit(solution)/shard_map/all_gather | solution.py:13
  217.9 8.3 %all-gather.2 = f32[8,1,8192]{2,1,0:T(1,128)S(1)} all-gather(f32[1,1,8192]{2,1,0:T(1,128)S(1)} %reshape.193), channel_id=1, replica_groups=mesh['row'=8,'col'=4] {'row'}, dimensions={0}, use_global_device_ids=true | all-gather | bytes 294912 | tf_op jit(solution)/shard_map/all_gather | solution.py:13
  227.3 31.2 %while.234 = (s32[]{:T(128)}, f32[1024]{0:T(1024)S(1)}, f32[1024]{0:T(1024)S(1)}, f32[2,4096]{1,0:T(2,128)S(1)}, f32[1024]{0:T(1024)S(1)}, /*index=5*/f32[2,4096...) while((s32[]{:T(128)}, f32[1024]{0:T(1024)S(1)}, ...), condition=%wide.region_35.36_spmd.clone, body=%wide.region_32.35_spmd.clone.sunk | while | flops 591401984 | bytes 34926708 | solution.py:54
  227.4 7.0 %fusion.88 = (f32[1024]{0:T(1024)S(1)}, f32[4096,1024]{1,0:T(8,128)}) fusion(f32[4096]{0:T(1024)S(1)} %bitcast.339, f32[1024]{0:T(1024)S(1)} %get-tuple-element.2130, f32[4096]{0:T(1024)S(1)} %bitcast.341, bf16[1024,64]{0,1:T(8,128)(2,1)S(1)} %get-tuple-element.2133, bf16[2,4096,64]{2,1,0:T(8,128)(2,1)S(1)} %get-tuple-element.2132, ...), kind=kOutput, calls=%fused_computation.84.clone.1 | convolution fusion | flops 562035712 | bytes 17997828 | tf_op jit(solution)/shard_map/while/body/eval_jaxpr/while/body/eval_jaxpr/ak,bk->ab/dot_general | solution.py:39
  234.4 8.5 %exponential_reduce_fusion.22 = f32[1024]{0:T(1024)S(1)} fusion(f32[4096,1024]{1,0:T(8,128)} %get-tuple-element.1931, f32[1024]{0:T(1024)S(1)} %select_maximum_fusion.10, f32[4096]{0:T(1024)S(1)} %bitcast.340, f32[1024]{0:T(1024)S(1)} %get-tuple-element.2130, f32[4096]{0:T(1024)S(1)} %bitcast.342), kind=kLoop, calls=%fused_computation.83.clone.1 | loop fusion | flops 29359104 | bytes 16822272 | tf_op jit(solution)/shard_map/while/body/eval_jaxpr/while/body/eval_jaxpr/reduce_sum | solution.py:45
  243.0 7.0 %fusion.88 = (f32[1024]{0:T(1024)S(1)}, f32[4096,1024]{1,0:T(8,128)}) fusion(f32[4096]{0:T(1024)S(1)} %bitcast.339, f32[1024]{0:T(1024)S(1)} %get-tuple-element.2130, f32[4096]{0:T(1024)S(1)} %bitcast.341, bf16[1024,64]{0,1:T(8,128)(2,1)S(1)} %get-tuple-element.2133, bf16[2,4096,64]{2,1,0:T(8,128)(2,1)S(1)} %get-tuple-element.2132, ...), kind=kOutput, calls=%fused_computation.84.clone.1 | convolution fusion | flops 562035712 | bytes 17997828 | tf_op jit(solution)/shard_map/while/body/eval_jaxpr/while/body/eval_jaxpr/ak,bk->ab/dot_general | solution.py:39
  250.0 8.5 %exponential_reduce_fusion.22 = f32[1024]{0:T(1024)S(1)} fusion(f32[4096,1024]{1,0:T(8,128)} %get-tuple-element.1931, f32[1024]{0:T(1024)S(1)} %select_maximum_fusion.10, f32[4096]{0:T(1024)S(1)} %bitcast.340, f32[1024]{0:T(1024)S(1)} %get-tuple-element.2130, f32[4096]{0:T(1024)S(1)} %bitcast.342), kind=kLoop, calls=%fused_computation.83.clone.1 | loop fusion | flops 29359104 | bytes 16822272 | tf_op jit(solution)/shard_map/while/body/eval_jaxpr/while/body/eval_jaxpr/reduce_sum | solution.py:45
  258.5 8.4 %pmax.30 = f32[1024]{0:T(1024)S(1)} all-reduce(f32[1024]{0:T(1024)S(1)} %get-tuple-element.1050), channel_id=1, replica_groups=mesh['row'=8,'col'=4] {'col'}, use_global_device_ids=true, to_apply=%region_36.37 | all-reduce | flops 1024 | bytes 8192 | tf_op jit(solution)/shard_map/pmax | solution.py:82
  266.9 10.4 %psum.46 = f32[1024]{0:T(1024)S(1)} all-reduce(f32[1024]{0:T(1024)S(1)} %exponential_multiply_fusion.1), channel_id=1, replica_groups=mesh['row'=8,'col'=4] {'col'}, use_global_device_ids=true, to_apply=%region_37.38 | all-reduce | flops 1024 | bytes 8192 | tf_op jit(solution)/shard_map/psum | solution.py:83
  277.3 26.6 %while.228 = (s32[]{:T(128)}, f32[8,1024]{1,0:T(8,128)S(1)}, f32[8,1024]{1,0:T(8,128)S(1)}, f32[1,1024]{1,0:T(1,128)S(1)}, bf16[8,1024,64]{2,1,0:T(8,128)(2,1)S(...) while((s32[]{:T(128)}, f32[8,1024]{1,0:T(8,128)S(1)}, ...), condition=%wide.region_42.43_spmd, body=%wide.region_38.42_spmd.sunk | while | flops 148045824 | bytes 9113709 | solution.py:57
  304.0 9.3 %all-gather.5 = f32[8,1,8192]{2,1,0:T(1,128)S(1)} all-gather(f32[1,1,8192]{2,1,0:T(1,128)S(1)} %reshape.199), channel_id=1, replica_groups=mesh['row'=8,'col'=4] {'row'}, dimensions={0}, use_global_device_ids=true | all-gather | bytes 294912 | tf_op jit(solution)/shard_map/all_gather | solution.py:13
  313.5 8.5 %all-gather.4 = f32[8,1,8192]{2,1,0:T(1,128)S(1)} all-gather(f32[1,1,8192]{2,1,0:T(1,128)S(1)} %reshape.197), channel_id=1, replica_groups=mesh['row'=8,'col'=4] {'row'}, dimensions={0}, use_global_device_ids=true | all-gather | bytes 294912 | tf_op jit(solution)/shard_map/all_gather | solution.py:13
  323.1 31.2 %while.235 = (s32[]{:T(128)}, f32[1024]{0:T(1024)S(1)}, f32[1024]{0:T(1024)S(1)}, f32[2,4096]{1,0:T(2,128)S(1)}, f32[1024]{0:T(1024)S(1)}, /*index=5*/f32[2,4096...) while((s32[]{:T(128)}, f32[1024]{0:T(1024)S(1)}, ...), condition=%wide.region_48.49_spmd.clone, body=%wide.region_45.48_spmd.clone.sunk | while | flops 591401984 | bytes 34926708 | solution.py:54
  323.2 7.0 %fusion.91 = (f32[1024]{0:T(1024)S(1)}, f32[4096,1024]{1,0:T(8,128)}) fusion(f32[4096]{0:T(1024)S(1)} %bitcast.343, f32[1024]{0:T(1024)S(1)} %get-tuple-element.2211, f32[4096]{0:T(1024)S(1)} %bitcast.345, bf16[1024,64]{0,1:T(8,128)(2,1)S(1)} %get-tuple-element.2214, bf16[2,4096,64]{2,1,0:T(8,128)(2,1)S(1)} %get-tuple-element.2213, ...), kind=kOutput, calls=%fused_computation.98.clone.1 | convolution fusion | flops 562035712 | bytes 17997828 | tf_op jit(solution)/shard_map/while/body/eval_jaxpr/while/body/eval_jaxpr/ak,bk->ab/dot_general | solution.py:39
  330.2 8.5 %exponential_reduce_fusion.23 = f32[1024]{0:T(1024)S(1)} fusion(f32[4096,1024]{1,0:T(8,128)} %get-tuple-element.1943, f32[1024]{0:T(1024)S(1)} %select_maximum_fusion.11, f32[4096]{0:T(1024)S(1)} %bitcast.344, f32[1024]{0:T(1024)S(1)} %get-tuple-element.2211, f32[4096]{0:T(1024)S(1)} %bitcast.346), kind=kLoop, calls=%fused_computation.97.clone.1 | loop fusion | flops 29359104 | bytes 16822272 | tf_op jit(solution)/shard_map/while/body/eval_jaxpr/while/body/eval_jaxpr/reduce_sum | solution.py:45
  338.8 7.0 %fusion.91 = (f32[1024]{0:T(1024)S(1)}, f32[4096,1024]{1,0:T(8,128)}) fusion(f32[4096]{0:T(1024)S(1)} %bitcast.343, f32[1024]{0:T(1024)S(1)} %get-tuple-element.2211, f32[4096]{0:T(1024)S(1)} %bitcast.345, bf16[1024,64]{0,1:T(8,128)(2,1)S(1)} %get-tuple-element.2214, bf16[2,4096,64]{2,1,0:T(8,128)(2,1)S(1)} %get-tuple-element.2213, ...), kind=kOutput, calls=%fused_computation.98.clone.1 | convolution fusion | flops 562035712 | bytes 17997828 | tf_op jit(solution)/shard_map/while/body/eval_jaxpr/while/body/eval_jaxpr/ak,bk->ab/dot_general | solution.py:39
  345.8 8.5 %exponential_reduce_fusion.23 = f32[1024]{0:T(1024)S(1)} fusion(f32[4096,1024]{1,0:T(8,128)} %get-tuple-element.1943, f32[1024]{0:T(1024)S(1)} %select_maximum_fusion.11, f32[4096]{0:T(1024)S(1)} %bitcast.344, f32[1024]{0:T(1024)S(1)} %get-tuple-element.2211, f32[4096]{0:T(1024)S(1)} %bitcast.346), kind=kLoop, calls=%fused_computation.97.clone.1 | loop fusion | flops 29359104 | bytes 16822272 | tf_op jit(solution)/shard_map/while/body/eval_jaxpr/while/body/eval_jaxpr/reduce_sum | solution.py:45
  354.3 8.4 %pmax.31 = f32[1024]{0:T(1024)S(1)} all-reduce(f32[1024]{0:T(1024)S(1)} %get-tuple-element.1056), channel_id=1, replica_groups=mesh['row'=8,'col'=4] {'col'}, use_global_device_ids=true, to_apply=%region_49.50 | all-reduce | flops 1024 | bytes 8192 | tf_op jit(solution)/shard_map/pmax | solution.py:82
  362.7 10.4 %psum.47 = f32[1024]{0:T(1024)S(1)} all-reduce(f32[1024]{0:T(1024)S(1)} %exponential_multiply_fusion), channel_id=1, replica_groups=mesh['row'=8,'col'=4] {'col'}, use_global_device_ids=true, to_apply=%region_50.51 | all-reduce | flops 1024 | bytes 8192 | tf_op jit(solution)/shard_map/psum | solution.py:83
  373.7 26.5 %while.230 = (s32[]{:T(128)}, f32[8,1024]{1,0:T(8,128)S(1)}, f32[8,1024]{1,0:T(8,128)S(1)}, f32[1,1024]{1,0:T(1,128)S(1)}, bf16[8,1024,64]{2,1,0:T(8,128)(2,1)S(...) while((s32[]{:T(128)}, f32[8,1024]{1,0:T(8,128)S(1)}, ...), condition=%wide.region_55.56_spmd, body=%wide.region_51.55_spmd.sunk | while | flops 148045824 | bytes 9113709 | solution.py:57
  400.3 9.3 %all-gather.7 = f32[8,1,8192]{2,1,0:T(1,128)S(1)} all-gather(f32[1,1,8192]{2,1,0:T(1,128)S(1)} %reshape.203), channel_id=1, replica_groups=mesh['row'=8,'col'=4] {'row'}, dimensions={0}, use_global_device_ids=true | all-gather | bytes 294912 | tf_op jit(solution)/shard_map/all_gather | solution.py:13
  409.8 8.3 %all-gather.6 = f32[8,1,8192]{2,1,0:T(1,128)S(1)} all-gather(f32[1,1,8192]{2,1,0:T(1,128)S(1)} %reshape.201), channel_id=1, replica_groups=mesh['row'=8,'col'=4] {'row'}, dimensions={0}, use_global_device_ids=true | all-gather | bytes 294912 | tf_op jit(solution)/shard_map/all_gather | solution.py:13
  (348 shorter events, 110.2 us)
Async XLA Ops:
  0.6 21.5 %copy-start.1 = (bf16[1024,64]{0,1:T(8,128)(2,1)S(1)}, bf16[1024,64]{0,1:T(8,128)(2,1)}, u32[]{:S(2)}) copy-start(bf16[1024,64]{0,1:T(8,128)(2,1)} %param.28) | copy-start | bytes 393220
  22.1 50.0 %copy-start.2 = (s32[1024]{0:T(1024)S(1)}, s32[1024]{0:T(1024)}, u32[]{:S(2)}) copy-start(s32[1024]{0:T(1024)} %param.30) | copy-start | bytes 12292
  86.1 45.5 %copy-start = (s32[8192]{0:T(1024)S(1)}, s32[8192]{0:T(1024)}, u32[]{:S(2)}) copy-start(s32[8192]{0:T(1024)} %param.31) | copy-start | bytes 98308
where the time goes:
time: 421 us; the launch traced here: 420 us
  blocking collectives  172 us (41%)
  other arithmetic  140 us (33%)
  matrix products  88.8 us (21%)
  local copies, waits for them, and re-layouts  12.7 us (3%)
    reduce_sum x40, other arithmetic, step_cols(): jnp.sum(jnp.exp(scores - newest[:, None]), axis=1)  125 us
    dot_general x40, matrix products, step_cols(): jnp.einsum('ak,bk->ab', pieces, cols_points, preferred_element_type=jnp.f...  88.8 us
    all_gather x8, blocking collectives, merged(): everything = jax.tree.map(lambda part: lax.all_gather(part, axis), value)  70.7 us
    psum x4, blocking collectives, on_device(): summed = lax.psum(summed * jnp.exp(highest - ceiling), 'col')  41.4 us
    pmax x4, blocking collectives, on_device(): ceiling = lax.pmax(highest, 'col')  33.6 us
    psum x1, blocking collectives, on_device(): donor_total = lax.psum(jnp.sum(donor_float), 'col')  14.1 us
    psum x1, blocking collectives, on_device(): treated_total = lax.psum(jnp.sum(treated_float), 'row')  12.4 us

commit v1 on v0

v1 whole, which is shorter than its diff:
```python
import functools
import math

import jax
import jax.numpy as jnp
from jax import lax
from jax.experimental import pallas as pl
from jax.experimental.pallas import tpu as pltpu
from jax.sharding import PartitionSpec as P

ITERS = 4
LOG2E = math.log2(math.e)
LN2 = math.log(2.0)
CH = 1024
LN = 128
KS = CH // LN
RB = 256
RV = 128
SHIFT = 20.0
MESH = pl.DeviceIdType.MESH
F32 = jnp.float32
BF16 = jnp.bfloat16


def split3(v):
    a = v.astype(BF16).astype(F32)
    r = v - a
    b = r.astype(BF16).astype(F32)
    return a, b, r - b


def kernel(nr, nc, x_ref, y_ref, tc_ref, dc_ref, f_ref, g_ref,
           xa, yt, e_ref, gam, m_ref, s_ref, om, q_ref, p_ref, u_ref, ysq, xsq,
           rbuf, cbuf, nbuf, mbuf, rs, rr, cs, cr, ns, nrv, ms, mr):
    rows = x_ref.shape[0]
    cols = y_ref.shape[0]
    dim = x_ref.shape[1]
    nch = cols // CH
    nrb = rows // RB
    rl = rows // LN
    me_r = lax.axis_index("row")
    me_c = lax.axis_index("col")
    row_peers = [lax.rem(me_r + d, nr) for d in range(1, nr)]
    col_peers = [lax.rem(me_c + d, nc) for d in range(1, nc)]

    barrier = pltpu.get_barrier_semaphore()
    for p in row_peers:
        pl.semaphore_signal(barrier, inc=1, device_id={"row": p}, device_id_type=MESH)
    for p in col_peers:
        pl.semaphore_signal(barrier, inc=1, device_id={"col": p}, device_id_type=MESH)

    def to_col(ref_at, send, recv):
        out = []
        for d, p in enumerate(col_peers):
            out.append(pltpu.make_async_remote_copy(
                src_ref=ref_at, dst_ref=ref_at, send_sem=send(d), recv_sem=recv(d),
                device_id={"col": p}, device_id_type=MESH))
        return out

    def to_row(ref_at, send, recv):
        out = []
        for d, p in enumerate(row_peers):
            out.append(pltpu.make_async_remote_copy(
                src_ref=ref_at, dst_ref=ref_at, send_sem=send(d), recv_sem=recv(d),
                device_id={"row": p}, device_id_type=MESH))
        return out

    tcf = tc_ref[...].astype(F32)
    dcf = dc_ref[...].astype(F32)
    xf = x_ref[...].astype(F32)
    c = xf * (4.0 * LOG2E)
    c1, c2, c3 = split3(c)
    ri = lax.broadcasted_iota(jnp.int32, (dim, 4 * dim), 0)
    ci = lax.broadcasted_iota(jnp.int32, (dim, 4 * dim), 1)
    wide = jnp.zeros((rows, 4 * dim), F32)
    for k, part in enumerate((c1, c2, c3)):
        place = (ri + k * dim == ci).astype(BF16)
        wide = wide + jnp.dot(part.astype(BF16), place, preferred_element_type=F32)
    lane = lax.broadcasted_iota(jnp.int32, (rows, 4 * dim), 1)
    wide = jnp.where((lane >= 3 * dim) & (lane < 3 * dim + 3), 1.0, wide)
    xa[...] = wide.astype(BF16)
    sq = jnp.broadcast_to(jnp.sum(xf * xf, axis=1, keepdims=True), (rows, LN))
    for r in range(rl):
        xsq[r:r + 1, :] = sq[r * LN:(r + 1) * LN, :].T[0:1, :]

    k1 = lax.broadcasted_iota(jnp.int32, (3 * dim, dim), 0)
    k2 = lax.broadcasted_iota(jnp.int32, (3 * dim, dim), 1)
    stack = (lax.rem(k1, dim) == k2).astype(BF16)

    def put_q(ch, q8):
        row = jnp.concatenate([q8[k:k + 1, :] for k in range(KS)], axis=1)
        a, b, cc = split3(row)
        r16 = lax.broadcasted_iota(jnp.int32, (16, CH), 0)
        val = jnp.where(r16 == 0, a, jnp.where(r16 == 1, b, jnp.where(r16 == 2, cc, jnp.where(r16 < 6, 1.0, 0.0))))
        yt[3 * dim:3 * dim + 16, pl.ds(pl.multiple_of(ch * CH, CH), CH)] = val.astype(BF16)

    def prep(ch, carry):
        js = pl.ds(pl.multiple_of(ch * CH, CH), CH)
        r8 = pl.ds(pl.multiple_of(ch * KS, KS), KS)
        t = lax.dot_general(stack, y_ref[js, :], (((1,), (1,)), ((), ())), preferred_element_type=F32)
        yt[0:3 * dim, js] = t.astype(BF16)
        yt[3 * dim + 16:4 * dim, js] = jnp.zeros((dim - 16, CH), BF16)
        t1 = t[0:dim, :]
        n2 = jnp.sum(t1 * t1, axis=0, keepdims=True)
        n8 = jnp.concatenate([n2[:, k * LN:(k + 1) * LN] for k in range(KS)], axis=0)
        ysq[r8, :] = n8
        q8 = jnp.log2(dc_ref[r8, :].astype(F32)) - (2.0 * LOG2E) * n8
        q_ref[r8, :] = q8
        put_q(ch, q8)
        return carry

    lax.fori_loop(0, nch, prep, 0)

    tsum = tcf[0:8, :]
    for r in range(1, rl // 8):
        tsum = tsum + tcf[r * 8:(r + 1) * 8, :]
    dsum = dcf[0:8, :]
    for r in range(1, cols // LN // 8):
        dsum = dsum + dcf[r * 8:(r + 1) * 8, :]
    mbuf[me_r] = tsum
    nbuf[me_c] = dsum

    pl.semaphore_wait(barrier, nr + nc - 2)
    n_copies = to_col(nbuf.at[me_c], lambda d: ns.at[d], lambda d: nrv.at[d])
    m_copies = to_row(mbuf.at[me_r], lambda d: ms.at[d], lambda d: mr.at[d])
    for cp in n_copies + m_copies:
        cp.start()

    def group(v, k):
        return v[:, k * LN:(k + 1) * LN]

    def score_rows(keep):
        m_ref[...] = jnp.full(m_ref.shape, -jnp.inf, F32)
        s_ref[...] = jnp.zeros(s_ref.shape, F32)

        def tile(step, carry):
            ch = step // nrb
            rb = step % nrb
            js = pl.ds(pl.multiple_of(ch * CH, CH), CH)
            rs_ = pl.ds(pl.multiple_of(rb * RB, RB), RB)
            sc = jnp.dot(xa[rs_, :], yt[:, js], preferred_element_type=F32)
            top = group(sc, 0)
            for k in range(1, KS):
                top = jnp.maximum(top, group(sc, k))
            old = m_ref[rs_, :]
            new = jnp.maximum(old, top)
            if keep:
                low = new - SHIFT
                gam[rs_, pl.ds(pl.multiple_of(ch * LN, LN), LN)] = new
            else:
                low = new
            tot = None
            for k in range(KS):
                ex = jnp.exp2(group(sc, k) - low)
                if keep:
                    e_ref[rs_, pl.ds(pl.multiple_of(ch * CH + k * LN, LN), LN)] = ex
                tot = ex if tot is None else tot + ex
            s_ref[rs_, :] = s_ref[rs_, :] * jnp.exp2(old - new) + tot
            m_ref[rs_, :] = new
            return carry

        lax.fori_loop(0, nch * nrb, tile, 0)

    def rows_dense_lse(it):
        for r in range(rl):
            mt = m_ref[r * LN:(r + 1) * LN, :].T
            st = s_ref[r * LN:(r + 1) * LN, :].T
            top = jnp.max(mt, axis=0, keepdims=True)
            tot = jnp.sum(st * jnp.exp2(mt - top), axis=0, keepdims=True)
            rbuf[it, me_c, r:r + 1, :] = top + jnp.log2(tot)

    def row_exchange(it):
        copies = to_col(rbuf.at[it, me_c], lambda d: rs.at[it, d], lambda d: rr.at[it, d])
        for cp in copies:
            cp.start()
        for cp in copies:
            cp.wait()

    def spread(v, r):
        return jnp.broadcast_to(v[r:r + 1, :], (LN, LN)).T

    def lse_merge(get, n):
        top = get(0)
        for k in range(1, n):
            top = jnp.maximum(top, get(k))
        tot = jnp.exp2(get(0) - top)
        for k in range(1, n):
            tot = tot + jnp.exp2(get(k) - top)
        return top + jnp.log2(tot)

    def sum_merge(get, n):
        tot = get(0)
        for k in range(1, n):
            tot = tot + get(k)
        return tot

    def send_cols(it, ch):
        part = cbuf.at[it, me_r, pl.ds(pl.multiple_of(ch * KS, KS), KS)]
        for cp in to_row(part, lambda d: cs.at[it, ch, d], lambda d: cr.at[it, ch, d]):
            cp.start()

    def wait_cols(it):
        def one(ch, carry):
            part = cbuf.at[it, me_r, pl.ds(pl.multiple_of(ch * KS, KS), KS)]
            for cp in to_row(part, lambda d: cs.at[it, ch, d], lambda d: cr.at[it, ch, d]):
                cp.wait()
            return carry
        lax.fori_loop(0, nch, one, 0)

    score_rows(False)
    rows_dense_lse(0)
    row_exchange(0)
    lsum = lse_merge(lambda k: rbuf[0, k], nc)
    p = jnp.log2(tcf) - lsum
    p_ref[...] = p
    l128 = lax.broadcasted_iota(jnp.int32, (LN, 2 * dim), 1)
    for r in range(rl):
        a, b, cc = split3(spread(p, r))
        half = xa[r * LN:(r + 1) * LN, 2 * dim:4 * dim].astype(F32)
        half = jnp.where(l128 == dim + 3, a, jnp.where(l128 == dim + 4, b, jnp.where(l128 == dim + 5, cc, half)))
        xa[r * LN:(r + 1) * LN, 2 * dim:4 * dim] = half.astype(BF16)

    def col_chunk(ch, carry):
        js = pl.ds(pl.multiple_of(ch * CH, CH), CH)

        def tile(rb, ms_):
            old, tot = ms_
            rs_ = pl.ds(pl.multiple_of(rb * RB, RB), RB)
            sc = jnp.dot(xa[rs_, :], yt[:, js], preferred_element_type=F32)
            sc = sc.reshape(RB // 8, 8, CH)
            new = jnp.maximum(old, jnp.max(sc, axis=0))
            ex = jnp.sum(jnp.exp2(sc - new[None]), axis=0)
            return new, tot * jnp.exp2(old - new) + ex

        top, tot = lax.fori_loop(
            0, nrb, tile, (jnp.full((8, CH), -jnp.inf, F32), jnp.zeros((8, CH), F32)))
        best = jnp.max(top, axis=0, keepdims=True)
        tot = jnp.sum(tot * jnp.exp2(top - best), axis=0, keepdims=True)
        val = best + jnp.log2(tot)
        cbuf[0, me_r, pl.ds(pl.multiple_of(ch * KS, KS), KS), :] = jnp.concatenate(
            [group(val, k) for k in range(KS)], axis=0)
        send_cols(0, ch)
        return carry

    lax.fori_loop(0, nch, col_chunk, 0)
    wait_cols(0)

    def new_q(ch, carry):
        r8 = pl.ds(pl.multiple_of(ch * KS, KS), KS)
        total = lse_merge(lambda k: cbuf[0, k, r8, :], nr)
        q8 = jnp.log2(dc_ref[r8, :].astype(F32)) + (q_ref[r8, :] - total)
        q_ref[r8, :] = q8
        put_q(ch, q8)
        return carry

    lax.fori_loop(0, nch, new_q, 0)

    score_rows(True)
    rows_dense_lse(1)
    row_exchange(1)
    lsum = lse_merge(lambda k: rbuf[1, k], nc) - SHIFT
    p_ref[...] = p_ref[...] - lsum
    for r in range(rl):
        rsl = slice(r * LN, (r + 1) * LN)
        lb = spread(lsum, r)
        for ch in range(nch):
            gam[rsl, ch * LN:(ch + 1) * LN] = jnp.exp2(gam[rsl, ch * LN:(ch + 1) * LN] + (SHIFT - lb))
        om[rsl, :] = spread(tcf, r)

    def sum_cols(it):
        def chunk(ch, carry):
            def tile(rv, acc):
                rs_ = pl.ds(pl.multiple_of(rv * RV, RV), RV)
                w = gam[rs_, pl.ds(pl.multiple_of(ch * LN, LN), LN)] * om[rs_, :]
                out = []
                for k in range(KS):
                    ex = e_ref[rs_, pl.ds(pl.multiple_of(ch * CH + k * LN, LN), LN)]
                    out.append(acc[k] + jnp.sum((ex * w).reshape(RV // 8, 8, LN), axis=0))
                return tuple(out)

            acc = lax.fori_loop(0, rows // RV, tile, tuple(jnp.zeros((8, LN), F32) for _ in range(KS)))
            val = jnp.concatenate([jnp.sum(a, axis=0, keepdims=True) for a in acc], axis=0)
            cbuf[it, me_r, pl.ds(pl.multiple_of(ch * KS, KS), KS), :] = val * (2.0 ** (-2 * SHIFT))
            send_cols(it, ch)
            return carry

        lax.fori_loop(0, nch, chunk, 0)
        wait_cols(it)
        return sum_merge(lambda k: cbuf[it, k], nr)

    def sum_rows(it):
        s_ref[...] = jnp.zeros(s_ref.shape, F32)

        def chunk(ch, carry):
            u8 = u_ref[pl.ds(pl.multiple_of(ch * KS, KS), KS), :]

            def tile(rv, carry2):
                rs_ = pl.ds(pl.multiple_of(rv * RV, RV), RV)
                tot = None
                for k in range(KS):
                    ex = e_ref[rs_, pl.ds(pl.multiple_of(ch * CH + k * LN, LN), LN)] * u8[k:k + 1, :]
                    tot = ex if tot is None else tot + ex
                s_ref[rs_, :] += tot * gam[rs_, pl.ds(pl.multiple_of(ch * LN, LN), LN)]
                return carry2

            return lax.fori_loop(0, rows // RV, tile, carry)

        lax.fori_loop(0, nch, chunk, 0)
        for r in range(rl):
            st = s_ref[r * LN:(r + 1) * LN, :].T
            rbuf[it, me_c, r:r + 1, :] = jnp.sum(st, axis=0, keepdims=True) * (2.0 ** (-2 * SHIFT))
        row_exchange(it)
        return sum_merge(lambda k: rbuf[it, k], nc)

    total = sum_cols(1)
    rsum = None
    for it in range(2, ITERS):
        u_ref[...] = dcf / total
        rsum = sum_rows(it)
        omega = tcf / rsum
        for r in range(rl):
            om[r * LN:(r + 1) * LN, :] = spread(omega, r)
        total = sum_cols(it)

    for cp in n_copies + m_copies:
        cp.wait()
    mall = jnp.log2(jnp.sum(sum_merge(lambda k: mbuf[k], nr), keepdims=True))
    nall = jnp.log2(jnp.sum(sum_merge(lambda k: nbuf[k], nc), keepdims=True))
    f_ref[...] = (0.5 * LN2) * (
        p_ref[...] - jnp.log2(rsum) + ITERS * nall - (ITERS - 1) * mall) + xsq[...]
    g_ref[...] = (0.5 * LN2) * (
        q_ref[...] - jnp.log2(total) + ITERS * (mall - nall)) + ysq[...]


def on_device(nr, nc, treated, donors, treated_counts, donor_counts):
    rows, dim = treated.shape
    cols = donors.shape[0]
    rl, cl, nch = rows // LN, cols // LN, cols // CH
    vm = pltpu.VMEM
    dma = pltpu.SemaphoreType.DMA
    f, g = pl.pallas_call(
        functools.partial(kernel, nr, nc),
        out_shape=(jax.ShapeDtypeStruct((rl, LN), F32), jax.ShapeDtypeStruct((cl, LN), F32)),
        in_specs=[pl.BlockSpec(memory_space=vm)] * 4,
        out_specs=(pl.BlockSpec(memory_space=vm), pl.BlockSpec(memory_space=vm)),
        scratch_shapes=[
            vm((rows, 4 * dim), BF16),
            vm((4 * dim, cols), BF16),
            vm((rows, cols), F32),
            vm((rows, nch * LN), F32),
            vm((rows, LN), F32),
            vm((rows, LN), F32),
            vm((rows, LN), F32),
            vm((cl, LN), F32),
            vm((rl, LN), F32),
            vm((cl, LN), F32),
            vm((cl, LN), F32),
            vm((rl, LN), F32),
            vm((ITERS, nc, rl, LN), F32),
            vm((ITERS, nr, cl, LN), F32),
            vm((nc, 8, LN), F32),
            vm((nr, 8, LN), F32),
            dma((ITERS, nc - 1)), dma((ITERS, nc - 1)),
            dma((ITERS, nch, nr - 1)), dma((ITERS, nch, nr - 1)),
            dma((nc - 1,)), dma((nc - 1,)),
            dma((nr - 1,)), dma((nr - 1,)),
        ],
        compiler_params=pltpu.CompilerParams(
            collective_id=0, has_side_effects=True, vmem_limit_bytes=60 * 1024 * 1024),
    )(treated, donors, treated_counts.reshape(rl, LN), donor_counts.reshape(cl, LN))
    return f.reshape(rows), g.reshape(cols)


def solution(mesh):
    in_specs = (P("row", None), P("col", None), P("row"), P("col"))
    out_specs = (P("row"), P("col"))
    return jax.shard_map(
        functools.partial(on_device, mesh.shape["row"], mesh.shape["col"]),
        mesh=mesh, in_specs=in_specs, out_specs=out_specs, check_vma=False,
    )
```

time: 421 us -> 123 us (0.29)
  blocking collectives: 172 us -> 0 us
  other arithmetic: 140 us -> 0 us
  Pallas kernels: 0 us -> 115 us
  matrix products: 88.8 us -> 0 us
  local copies, waits for them, and re-layouts: 12.7 us -> 7.18 us
    reduce_sum x76 -> x0, other arithmetic: 137 us -> none  [the longest x40 125 us: step_cols(): jnp.sum(jnp.exp(scores - newest[:, None]), axis=1)]
    pallas_call x0 -> x1, Pallas kernels: none -> 115 us  [on_device(): pl.pallas_call(functools.partial(kernel, nr, nc), out_shape=(jax.ShapeDty...]
    dot_general x40 -> x0, matrix products: 88.8 us -> none  [step_cols(): jnp.einsum('ak,bk->ab', pieces, cols_points, preferred_element_type=jnp.f...]
    all_gather x8 -> x0, blocking collectives: 70.7 us -> none  [merged(): everything = jax.tree.map(lambda part: lax.all_gather(part, axis), value)]
    psum x6 -> x0, blocking collectives: 68 us -> none  [the longest x4 41.4 us: on_device(): summed = lax.psum(summed * jnp.exp(highest - ceiling), 'col')]
    pmax x4 -> x0, blocking collectives: 33.6 us -> none  [on_device(): ceiling = lax.pmax(highest, 'col')]
    dynamic_update_slice x64 -> x0, local copies, waits for them, and re-layouts: 6.94 us -> none  [partial_soft(): lax.map(one_rows, points.reshape(rows_here // row_block, row_block, width...]
where the time goes in v1:
time: 123 us
  Pallas kernels  115 us (93%)
  local copies, waits for them, and re-layouts  7.18 us (6%)
    pallas_call x1, Pallas kernels, on_device(): pl.pallas_call(functools.partial(kernel, nr, nc), out_shape=(jax.ShapeDty...  115 us
    unnamed x4, local copies, waits for them, and re-layouts  7.18 us

profile of v1, /device:TPU:0, one launch (start us, length us, event | category | flops | bytes accessed | tf_op | source)
XLA Modules:
  0.0 122.9 jit_solution(11490536698391033266)
XLA Ops:
  0.6 1.8 %copy.6.x_ref = bf16[1024,64]{1,0:T(8,128)(2,1)} copy(bf16[1024,64]{0,1:T(8,128)(2,1)} %param.4) | data formatting | bytes 262144 | tf_op args[0]
  2.4 2.8 %copy.7.y_ref = bf16[8192,64]{1,0:T(8,128)(2,1)} copy(bf16[8192,64]{0,1:T(8,128)(2,1)} %param.5) | data formatting | bytes 2097152 | tf_op args[1]
  5.2 115.0 %shard_map.59 = (f32[8,128]{1,0:T(8,128)}, f32[64,128]{1,0:T(8,128)}) custom-call(bf16[1024,64]{1,0:T(8,128)(2,1)} %copy.6.x_ref, bf16[8192,64]{1,0:T(8,128)(2,1)} %copy.7.y_ref, s32[8,128]{1,0:T(8,128)} %bitcast.6, s32[64,128]{1,0:T(8,128)} %bitcast.4), custom_call_target="tpu_custom_call" | custom-call | tf_op jit(solution)/shard_map/pallas_call | solution.py:341
  120.2 1.3 %copy.10 = f32[1024]{0:T(1024)} copy(f32[1024]{0:T(1024)} %bitcast.7) | data formatting | bytes 8192
  121.5 1.4 %copy.11 = f32[8192]{0:T(1024)} copy(f32[8192]{0:T(1024)} %bitcast.5) | data formatting | bytes 65536

commit v2 on v1

--- a/solution.py
+++ b/solution.py
@@ -17,6 +17,9 @@
 RB = 256
 RV = 128
 SHIFT = 20.0
+UR = 4
+UC = 4
+US = 8
 MESH = pl.DeviceIdType.MESH
 F32 = jnp.float32
 BF16 = jnp.bfloat16
@@ -32,9 +35,8 @@
 def kernel(nr, nc, x_ref, y_ref, tc_ref, dc_ref, f_ref, g_ref,
            xa, yt, e_ref, gam, m_ref, s_ref, om, q_ref, p_ref, u_ref, ysq, xsq,
            rbuf, cbuf, nbuf, mbuf, rs, rr, cs, cr, ns, nrv, ms, mr):
-    rows = x_ref.shape[0]
-    cols = y_ref.shape[0]
-    dim = x_ref.shape[1]
+    dim, rows = x_ref.shape
+    cols = y_ref.shape[1]
     nch = cols // CH
     nrb = rows // RB
     rl = rows // LN
@@ -75,17 +77,14 @@
     wide = jnp.zeros((rows, 4 * dim), F32)
     for k, part in enumerate((c1, c2, c3)):
         place = (ri + k * dim == ci).astype(BF16)
-        wide = wide + jnp.dot(part.astype(BF16), place, preferred_element_type=F32)
+        wide = wide + lax.dot_general(
+            part.astype(BF16), place, (((0,), (0,)), ((), ())), preferred_element_type=F32)
     lane = lax.broadcasted_iota(jnp.int32, (rows, 4 * dim), 1)
     wide = jnp.where((lane >= 3 * dim) & (lane < 3 * dim + 3), 1.0, wide)
     xa[...] = wide.astype(BF16)
-    sq = jnp.broadcast_to(jnp.sum(xf * xf, axis=1, keepdims=True), (rows, LN))
+    sq = jnp.sum(xf * xf, axis=0, keepdims=True)
     for r in range(rl):
-        xsq[r:r + 1, :] = sq[r * LN:(r + 1) * LN, :].T[0:1, :]
-
-    k1 = lax.broadcasted_iota(jnp.int32, (3 * dim, dim), 0)
-    k2 = lax.broadcasted_iota(jnp.int32, (3 * dim, dim), 1)
-    stack = (lax.rem(k1, dim) == k2).astype(BF16)
+        xsq[r:r + 1, :] = sq[:, r * LN:(r + 1) * LN]
 
     def put_q(ch, q8):
         row = jnp.concatenate([q8[k:k + 1, :] for k in range(KS)], axis=1)
@@ -97,10 +96,11 @@
     def prep(ch, carry):
         js = pl.ds(pl.multiple_of(ch * CH, CH), CH)
         r8 = pl.ds(pl.multiple_of(ch * KS, KS), KS)
-        t = lax.dot_general(stack, y_ref[js, :], (((1,), (1,)), ((), ())), preferred_element_type=F32)
-        yt[0:3 * dim, js] = t.astype(BF16)
+        yc = y_ref[:, js]
+        for k in range(3):
+            yt[k * dim:(k + 1) * dim, js] = yc
         yt[3 * dim + 16:4 * dim, js] = jnp.zeros((dim - 16, CH), BF16)
-        t1 = t[0:dim, :]
+        t1 = yc.astype(F32)
         n2 = jnp.sum(t1 * t1, axis=0, keepdims=True)
         n8 = jnp.concatenate([n2[:, k * LN:(k + 1) * LN] for k in range(KS)], axis=0)
         ysq[r8, :] = n8
@@ -159,7 +159,7 @@
             m_ref[rs_, :] = new
             return carry
 
-        lax.fori_loop(0, nch * nrb, tile, 0)
+        lax.fori_loop(0, nch * nrb, tile, 0, unroll=UR)
 
     def rows_dense_lse(it):
         for r in range(rl):
@@ -194,18 +194,20 @@
             tot = tot + get(k)
         return tot
 
-    def send_cols(it, ch):
-        part = cbuf.at[it, me_r, pl.ds(pl.multiple_of(ch * KS, KS), KS)]
-        for cp in to_row(part, lambda d: cs.at[it, ch, d], lambda d: cr.at[it, ch, d]):
-            cp.start()
-
-    def wait_cols(it):
-        def one(ch, carry):
-            part = cbuf.at[it, me_r, pl.ds(pl.multiple_of(ch * KS, KS), KS)]
-            for cp in to_row(part, lambda d: cs.at[it, ch, d], lambda d: cr.at[it, ch, d]):
+    cuts = (0, nch * 3 // 4, nch)
+
+    def col_copies(it, n):
+        part = cbuf.at[it, me_r, cuts[n] * KS:cuts[n + 1] * KS]
+        return to_row(part, lambda d: cs.at[it, n, d], lambda d: cr.at[it, n, d])
+
+    def over_chunks(it, chunk):
+        for n in range(2):
+            lax.fori_loop(cuts[n], cuts[n + 1], chunk, 0)
+            for cp in col_copies(it, n):
+                cp.start()
+        for n in range(2):
+            for cp in col_copies(it, n):
                 cp.wait()
-            return carry
-        lax.fori_loop(0, nch, one, 0)
 
     score_rows(False)
     rows_dense_lse(0)
@@ -233,17 +235,15 @@
             return new, tot * jnp.exp2(old - new) + ex
 
         top, tot = lax.fori_loop(
-            0, nrb, tile, (jnp.full((8, CH), -jnp.inf, F32), jnp.zeros((8, CH), F32)))
+            0, nrb, tile, (jnp.full((8, CH), -jnp.inf, F32), jnp.zeros((8, CH), F32)), unroll=UC)
         best = jnp.max(top, axis=0, keepdims=True)
         tot = jnp.sum(tot * jnp.exp2(top - best), axis=0, keepdims=True)
         val = best + jnp.log2(tot)
         cbuf[0, me_r, pl.ds(pl.multiple_of(ch * KS, KS), KS), :] = jnp.concatenate(
             [group(val, k) for k in range(KS)], axis=0)
-        send_cols(0, ch)
         return carry
 
-    lax.fori_loop(0, nch, col_chunk, 0)
-    wait_cols(0)
+    over_chunks(0, col_chunk)
 
     def new_q(ch, carry):
         r8 = pl.ds(pl.multiple_of(ch * KS, KS), KS)
@@ -278,14 +278,12 @@
                     out.append(acc[k] + jnp.sum((ex * w).reshape(RV // 8, 8, LN), axis=0))
                 return tuple(out)
 
-            acc = lax.fori_loop(0, rows // RV, tile, tuple(jnp.zeros((8, LN), F32) for _ in range(KS)))
+            acc = lax.fori_loop(0, rows // RV, tile, tuple(jnp.zeros((8, LN), F32) for _ in range(KS)), unroll=US)
             val = jnp.concatenate([jnp.sum(a, axis=0, keepdims=True) for a in acc], axis=0)
             cbuf[it, me_r, pl.ds(pl.multiple_of(ch * KS, KS), KS), :] = val * (2.0 ** (-2 * SHIFT))
-            send_cols(it, ch)
             return carry
 
-        lax.fori_loop(0, nch, chunk, 0)
-        wait_cols(it)
+        over_chunks(it, chunk)
         return sum_merge(lambda k: cbuf[it, k], nr)
 
     def sum_rows(it):
@@ -303,7 +301,7 @@
                 s_ref[rs_, :] += tot * gam[rs_, pl.ds(pl.multiple_of(ch * LN, LN), LN)]
                 return carry2
 
-            return lax.fori_loop(0, rows // RV, tile, carry)
+            return lax.fori_loop(0, rows // RV, tile, carry, unroll=US)
 
         lax.fori_loop(0, nch, chunk, 0)
         for r in range(rl):
@@ -361,13 +359,13 @@
             vm((nc, 8, LN), F32),
             vm((nr, 8, LN), F32),
             dma((ITERS, nc - 1)), dma((ITERS, nc - 1)),
-            dma((ITERS, nch, nr - 1)), dma((ITERS, nch, nr - 1)),
+            dma((ITERS, 2, nr - 1)), dma((ITERS, 2, nr - 1)),
             dma((nc - 1,)), dma((nc - 1,)),
             dma((nr - 1,)), dma((nr - 1,)),
         ],
         compiler_params=pltpu.CompilerParams(
             collective_id=0, has_side_effects=True, vmem_limit_bytes=60 * 1024 * 1024),
-    )(treated, donors, treated_counts.reshape(rl, LN), donor_counts.reshape(cl, LN))
+    )(treated.T, donors.T, treated_counts.reshape(rl, LN), donor_counts.reshape(cl, LN))
     return f.reshape(rows), g.reshape(cols)
 
 

time: 123 us -> 97.6 us (0.79)
  Pallas kernels: 115 us -> 94 us
  local copies, waits for them, and re-layouts: 7.18 us -> 2.63 us
    pallas_call x1, Pallas kernels: 115 us -> 94 us  [on_device(): pl.pallas_call(functools.partial(kernel, nr, nc), out_shape=(jax.ShapeDty...]
    unnamed x4, local copies, waits for them, and re-layouts: 7.18 us -> 2.63 us
where the time goes in v2:
time: 97.6 us; the launch traced here: 97.3 us
  Pallas kernels  94 us (96%)
  local copies, waits for them, and re-layouts  2.63 us (3%)
    pallas_call x1, Pallas kernels, on_device(): pl.pallas_call(functools.partial(kernel, nr, nc), out_shape=(jax.ShapeDty...  94 us
    unnamed x4, local copies, waits for them, and re-layouts  2.63 us

profile of v2, /device:TPU:0, one launch (start us, length us, event | category | flops | bytes accessed | tf_op | source)
XLA Modules:
  0.0 97.3 jit_solution(390150004318515988)
XLA Ops:
  0.6 94.0 %shard_map.59 = (f32[8,128]{1,0:T(8,128)}, f32[64,128]{1,0:T(8,128)}) custom-call(bf16[64,1024]{1,0:T(8,128)(2,1)} %bitcast.7, bf16[64,8192]{1,0:T(8,128)(2,1)} %bitcast.6, s32[8,128]{1,0:T(8,128)} %bitcast.10, s32[64,128]{1,0:T(8,128)} %bitcast.8), custom_call_target="tpu_custom_call" | custom-call | tf_op jit(solution)/shard_map/pallas_call | solution.py:339
  94.7 0.0 copy-start
  94.7 0.7 copy-done
  95.4 0.6 copy.8
  95.9 1.4 %copy.9 = f32[8192]{0:T(1024)} copy(f32[8192]{0:T(1024)} %bitcast.9) | data formatting | bytes 65536
Async XLA Ops:
  94.7 0.7 copy-start

commit v3 on v2

--- a/solution.py
+++ b/solution.py
@@ -19,7 +19,7 @@
 SHIFT = 20.0
 UR = 4
 UC = 4
-US = 8
+US = 4
 MESH = pl.DeviceIdType.MESH
 F32 = jnp.float32
 BF16 = jnp.bfloat16
@@ -40,6 +40,8 @@
     nch = cols // CH
     nrb = rows // RB
     rl = rows // LN
+    hrl = rl // 2
+    cuts = (0, nch // 2, nch)
     me_r = lax.axis_index("row")
     me_c = lax.axis_index("col")
     row_peers = [lax.rem(me_r + d, nr) for d in range(1, nr)]
@@ -129,7 +131,7 @@
     def group(v, k):
         return v[:, k * LN:(k + 1) * LN]
 
-    def score_rows(keep):
+    def score_rows(keep, before):
         m_ref[...] = jnp.full(m_ref.shape, -jnp.inf, F32)
         s_ref[...] = jnp.zeros(s_ref.shape, F32)
 
@@ -159,7 +161,9 @@
             m_ref[rs_, :] = new
             return carry
 
-        lax.fori_loop(0, nch * nrb, tile, 0, unroll=UR)
+        for n in range(2):
+            before(n)
+            lax.fori_loop(cuts[n] * nrb, cuts[n + 1] * nrb, tile, 0, unroll=UR)
 
     def rows_dense_lse(it):
         for r in range(rl):
@@ -170,7 +174,7 @@
             rbuf[it, me_c, r:r + 1, :] = top + jnp.log2(tot)
 
     def row_exchange(it):
-        copies = to_col(rbuf.at[it, me_c], lambda d: rs.at[it, d], lambda d: rr.at[it, d])
+        copies = to_col(rbuf.at[it, me_c], lambda d: rs.at[it, 0, d], lambda d: rr.at[it, 0, d])
         for cp in copies:
             cp.start()
         for cp in copies:
@@ -194,7 +198,6 @@
             tot = tot + get(k)
         return tot
 
-    cuts = (0, nch * 3 // 4, nch)
 
     def col_copies(it, n):
         part = cbuf.at[it, me_r, cuts[n] * KS:cuts[n + 1] * KS]
@@ -205,11 +208,12 @@
             lax.fori_loop(cuts[n], cuts[n + 1], chunk, 0)
             for cp in col_copies(it, n):
                 cp.start()
-        for n in range(2):
-            for cp in col_copies(it, n):
-                cp.wait()
-
-    score_rows(False)
+
+    def wait_group(it, n):
+        for cp in col_copies(it, n):
+            cp.wait()
+
+    score_rows(False, lambda n: None)
     rows_dense_lse(0)
     row_exchange(0)
     lsum = lse_merge(lambda k: rbuf[0, k], nc)
@@ -253,9 +257,11 @@
         put_q(ch, q8)
         return carry
 
-    lax.fori_loop(0, nch, new_q, 0)
-
-    score_rows(True)
+    def take_q(n):
+        wait_group(0, n)
+        lax.fori_loop(cuts[n], cuts[n + 1], new_q, 0)
+
+    score_rows(True, take_q)
     rows_dense_lse(1)
     row_exchange(1)
     lsum = lse_merge(lambda k: rbuf[1, k], nc) - SHIFT
@@ -267,8 +273,14 @@
             gam[rsl, ch * LN:(ch + 1) * LN] = jnp.exp2(gam[rsl, ch * LN:(ch + 1) * LN] + (SHIFT - lb))
         om[rsl, :] = spread(tcf, r)
 
-    def sum_cols(it):
-        def chunk(ch, carry):
+    per = rows // RV // 2
+
+    def half_copies(it, h):
+        part = rbuf.at[it, me_c, h * hrl:(h + 1) * hrl]
+        return to_col(part, lambda d: rs.at[it, h, d], lambda d: rr.at[it, h, d])
+
+    def sum_cols(it, before):
+        def chunk_of(h, ch):
             def tile(rv, acc):
                 rs_ = pl.ds(pl.multiple_of(rv * RV, RV), RV)
                 w = gam[rs_, pl.ds(pl.multiple_of(ch * LN, LN), LN)] * om[rs_, :]
@@ -278,18 +290,28 @@
                     out.append(acc[k] + jnp.sum((ex * w).reshape(RV // 8, 8, LN), axis=0))
                 return tuple(out)
 
-            acc = lax.fori_loop(0, rows // RV, tile, tuple(jnp.zeros((8, LN), F32) for _ in range(KS)), unroll=US)
+            acc = lax.fori_loop(h * per, (h + 1) * per, tile, tuple(jnp.zeros((8, LN), F32) for _ in range(KS)), unroll=US)
             val = jnp.concatenate([jnp.sum(a, axis=0, keepdims=True) for a in acc], axis=0)
-            cbuf[it, me_r, pl.ds(pl.multiple_of(ch * KS, KS), KS), :] = val * (2.0 ** (-2 * SHIFT))
+            return val * (2.0 ** (-2 * SHIFT))
+
+        def first(ch, carry):
+            cbuf[it, me_r, pl.ds(pl.multiple_of(ch * KS, KS), KS), :] = chunk_of(0, ch)
             return carry
 
-        over_chunks(it, chunk)
-        return sum_merge(lambda k: cbuf[it, k], nr)
+        def second(ch, carry):
+            r8 = pl.ds(pl.multiple_of(ch * KS, KS), KS)
+            cbuf[it, me_r, r8, :] = cbuf[it, me_r, r8, :] + chunk_of(1, ch)
+            return carry
+
+        before(0)
+        lax.fori_loop(0, nch, first, 0)
+        before(1)
+        over_chunks(it, second)
 
     def sum_rows(it):
         s_ref[...] = jnp.zeros(s_ref.shape, F32)
 
-        def chunk(ch, carry):
+        def over(h, ch, carry):
             u8 = u_ref[pl.ds(pl.multiple_of(ch * KS, KS), KS), :]
 
             def tile(rv, carry2):
@@ -301,24 +323,38 @@
                 s_ref[rs_, :] += tot * gam[rs_, pl.ds(pl.multiple_of(ch * LN, LN), LN)]
                 return carry2
 
-            return lax.fori_loop(0, rows // RV, tile, carry, unroll=US)
-
-        lax.fori_loop(0, nch, chunk, 0)
-        for r in range(rl):
-            st = s_ref[r * LN:(r + 1) * LN, :].T
-            rbuf[it, me_c, r:r + 1, :] = jnp.sum(st, axis=0, keepdims=True) * (2.0 ** (-2 * SHIFT))
-        row_exchange(it)
-        return sum_merge(lambda k: rbuf[it, k], nc)
-
-    total = sum_cols(1)
-    rsum = None
+            return lax.fori_loop(h * per, (h + 1) * per, tile, carry, unroll=US)
+
+        for n in range(2):
+            wait_group(it - 1, n)
+            sl = slice(cuts[n] * KS, cuts[n + 1] * KS)
+            u_ref[sl, :] = dcf[sl, :] / sum_merge(lambda k: cbuf[it - 1, k, sl, :], nr)
+            for h in range(2):
+                lax.fori_loop(cuts[n], cuts[n + 1], functools.partial(over, h), 0)
+                if n == 1:
+                    for r in range(h * hrl, (h + 1) * hrl):
+                        st = s_ref[r * LN:(r + 1) * LN, :].T
+                        rbuf[it, me_c, r:r + 1, :] = jnp.sum(st, axis=0, keepdims=True) * (2.0 ** (-2 * SHIFT))
+                    for cp in half_copies(it, h):
+                        cp.start()
+
+    sum_cols(1, lambda h: None)
     for it in range(2, ITERS):
-        u_ref[...] = dcf / total
-        rsum = sum_rows(it)
-        omega = tcf / rsum
-        for r in range(rl):
-            om[r * LN:(r + 1) * LN, :] = spread(omega, r)
-        total = sum_cols(it)
+        sum_rows(it)
+
+        def weights(h, it=it):
+            for cp in half_copies(it, h):
+                cp.wait()
+            sl = slice(h * hrl, (h + 1) * hrl)
+            omega = tcf[sl, :] / sum_merge(lambda k: rbuf[it, k, sl, :], nc)
+            for r in range(hrl):
+                om[(h * hrl + r) * LN:(h * hrl + r + 1) * LN, :] = spread(omega, r)
+
+        sum_cols(it, weights)
+    for n in range(2):
+        wait_group(ITERS - 1, n)
+    total = sum_merge(lambda k: cbuf[ITERS - 1, k], nr)
+    rsum = sum_merge(lambda k: rbuf[ITERS - 1, k], nc)
 
     for cp in n_copies + m_copies:
         cp.wait()
@@ -358,7 +394,7 @@
             vm((ITERS, nr, cl, LN), F32),
             vm((nc, 8, LN), F32),
             vm((nr, 8, LN), F32),
-            dma((ITERS, nc - 1)), dma((ITERS, nc - 1)),
+            dma((ITERS, 2, nc - 1)), dma((ITERS, 2, nc - 1)),
             dma((ITERS, 2, nr - 1)), dma((ITERS, 2, nr - 1)),
             dma((nc - 1,)), dma((nc - 1,)),
             dma((nr - 1,)), dma((nr - 1,)),

time: 97.6 us -> 91.2 us (0.934)
  Pallas kernels: 94 us -> 87.7 us
    pallas_call x1, Pallas kernels: 94 us -> 87.7 us  [on_device(): pl.pallas_call(functools.partial(kernel, nr, nc), out_shape=(jax.ShapeDty...]
where the time goes in v3:
time: 91.2 us; the launch traced here: 91 us
  Pallas kernels  87.7 us (96%)
  local copies, waits for them, and re-layouts  2.63 us (3%)
    pallas_call x1, Pallas kernels, on_device(): pl.pallas_call(functools.partial(kernel, nr, nc), out_shape=(jax.ShapeDty...  87.7 us
    unnamed x4, local copies, waits for them, and re-layouts  2.63 us

profile of v3, /device:TPU:0, one launch (start us, length us, event | category | flops | bytes accessed | tf_op | source)
XLA Modules:
  0.0 91.0 jit_solution(4990894193702067234)
XLA Ops:
  0.6 87.7 %shard_map.59 = (f32[8,128]{1,0:T(8,128)}, f32[64,128]{1,0:T(8,128)}) custom-call(bf16[64,1024]{1,0:T(8,128)(2,1)} %bitcast.7, bf16[64,8192]{1,0:T(8,128)(2,1)} %bitcast.6, s32[8,128]{1,0:T(8,128)} %bitcast.10, s32[64,128]{1,0:T(8,128)} %bitcast.8), custom_call_target="tpu_custom_call" | custom-call | tf_op jit(solution)/shard_map/pallas_call | solution.py:375
  88.3 0.0 copy-start
  88.3 0.7 copy-done
  89.0 0.6 copy.8
  89.6 1.4 %copy.9 = f32[8192]{0:T(1024)} copy(f32[8192]{0:T(1024)} %bitcast.9) | data formatting | bytes 65536
Async XLA Ops:
  88.3 0.7 copy-start
